TPU v7x, 32 devices: a whole 2x2x4 slice. The times are simulated.
32 devices in a mesh: section: 8 (over z, x), dp: 4 (over y, core).
Axes of the slice: x: 2, y: 2, z: 4, core: 2. Of those that a mesh axis runs over, the one named last changes fastest.
Arguments:
- states: bfloat16 [4, 8, 32, 4096], P('dp', 'section'), may hold values from -8 to 8
- memory: bfloat16 [4, 8, 2, 128, 4096], P('dp', 'section'), may hold values from -12 to 12
- memory_len: int32 [4, 8], P('dp', 'section'), may hold values from 2 to 128
- decode_len: int32 [4, 8], P('dp', 'section'), may hold values from 1 to 32
- owner_map: int32 [8], replicated, may hold values from 0 to 7, as said below
- section_gain: bfloat16 [8, 4096], P('section'), may hold values from 0.5 to 2
- cotangent: bfloat16 [4, 3, 8, 32, 4096], P('dp', None, 'section'), may hold values from -18 to 18
Outputs:
- final_states: bfloat16 [4, 8, 32, 4096], P('dp', 'section')
- gain_grad: float32 [8, 4096], P('section')
Inputs may be any that keep to these rules, and one draw needn't show every extreme that they name: owner_map[m] = (m + c) mod 8 for one offset c from 3 to 7, the same for all m.
All inputs are finite; a program needn't handle non-finite values.
Results may differ from a plain program's by a relative error of at most 0.0085.
Values may be sent and summed in bfloat16 or wider, within the bound.
A program may use at most 64 MiB of HBM per device.

v0:
```python
import functools

import jax
import jax.numpy as jnp
from jax import lax
from jax.experimental import pallas as pl
from jax.experimental.pallas import tpu as pltpu
from jax.sharding import PartitionSpec as P

HD = 256
STEPS = 3
MESH = pl.DeviceIdType.MESH


WITH, LEFT, CAME = range(3)
PLANS = {
    3: ((0.5, 0.5, 0.5), (LEFT, CAME, CAME)),
    4: ((0.5, 0.5, 0), (LEFT, LEFT, WITH)),
    5: ((1, 0, 0), (WITH, WITH, LEFT)),
    6: ((0.5, 0.5, 0.5), (LEFT, CAME, LEFT)),
    7: ((1, 0, 0), (WITH, WITH, LEFT)),
}
OTHER = PLANS[4]


def window_kernel(
    offset, sections, replicas,
    states, memory, memory_len, decode_len, gain, cotangent,
    final, grad,
    kv, held, cots, own_cots, mixed, arrived, note, notes, rows_f32, part, parts, own, slots,
    kv_sem, own_sem, x_send, x_recv, cot_send, cot_recv, mixed_send, mixed_recv,
    note_send, note_recv, part_send, part_recv, final_send, final_recv, slot_send, slot_recv,
):
    me = lax.axis_index("section")
    rep = lax.axis_index("dp")
    heads = held.shape[1] // HD
    dec = held.shape[0]
    enc = kv.shape[1]
    shares_out, moments = PLANS[offset] if sections == 8 else OTHER
    outs = [int(share * heads) for share in shares_out]

    def cots_sent(moment):
        return [t for t in sorted(cot_copies, reverse=True) if moments[t] == moment]

    def section_at(shift):
        return {"section": lax.rem(me + shift % sections, sections)}

    def to_section(src, dst, send, recv, shift):
        return pltpu.make_async_remote_copy(
            src_ref=src, dst_ref=dst, send_sem=send, recv_sem=recv,
            device_id=section_at(shift), device_id_type=MESH,
        )

    barrier = pltpu.get_barrier_semaphore()
    shifts = sorted({s % sections for t in range(STEPS) for s in (offset - t, t - offset)})
    for shift in shifts:
        pl.semaphore_signal(barrier, inc=1, device_id=section_at(shift), device_id_type=MESH)

    def greet(j, carry):
        pl.semaphore_signal(
            barrier, inc=1, device_id={"dp": lax.rem(rep + j, replicas)}, device_id_type=MESH
        )
        return carry

    lax.fori_loop(1, replicas, greet, 0)

    kv_copy = pltpu.make_async_copy(memory.at[0, 0], kv, kv_sem)
    kv_copy.start()

    for h in range(heads):
        rows_f32[h : h + 1, :] = gain[:, h * HD : (h + 1) * HD].astype(jnp.float32)
    rows_f32[heads:, :] = jnp.full((heads, HD), decode_len[0, 0], jnp.int32).astype(jnp.float32)
    note[...] = rows_f32[...].astype(jnp.bfloat16)

    x_copy = to_section(states.at[0, 0], held, x_send, x_recv, offset)
    note_copies = [
        to_section(note, notes.at[t], note_send.at[t], note_recv.at[t], offset - t)
        for t in range(STEPS)
    ]
    cot_copies, own_copies, mixed_copies, part_copies = {}, {}, {}, {}
    for t in range(STEPS):
        out = pl.ds(0, outs[t] * HD)
        rest = pl.ds(outs[t] * HD, (heads - outs[t]) * HD)
        rows = pl.ds(outs[t], heads - outs[t])
        if outs[t] > 0:
            own_copies[t] = pltpu.make_async_copy(
                cotangent.at[0, t, 0, :, out], own_cots.at[t, :, out], own_sem.at[t]
            )
            mixed_copies[t] = to_section(
                mixed.at[t, :, out], arrived.at[t, :, out],
                mixed_send.at[t], mixed_recv.at[t], t - offset,
            )
        if outs[t] < heads:
            cot_copies[t] = to_section(
                cotangent.at[0, t, 0, :, rest], cots.at[t, :, rest],
                cot_send.at[t], cot_recv.at[t], offset - t,
            )
            part_copies[t] = to_section(
                part.at[t, rows], parts.at[t, rows], part_send.at[t], part_recv.at[t], t - offset
            )
    final_copy = to_section(held, final.at[0, 0], final_send, final_recv, STEPS - 1 - offset)

    pl.semaphore_wait(barrier, len(shifts) + replicas - 1)
    x_copy.start()
    for copy in note_copies:
        copy.start()
    for t in cots_sent(WITH):
        cot_copies[t].start()
    for copy in own_copies.values():
        copy.start()
    x_copy.wait_send()
    for t in cots_sent(LEFT):
        cot_copies[t].start()

    kv_copy.wait()
    for copy in note_copies:
        copy.wait_recv()
    x_copy.wait_recv()
    for t in cots_sent(CAME):
        cot_copies[t].start()

    row = lax.broadcasted_iota(jnp.int32, (dec, HD), 0).astype(jnp.float32)
    live = row < notes[0].astype(jnp.float32)[heads : heads + 1, :]
    key_live = lax.broadcasted_iota(jnp.int32, (dec, enc), 1) < memory_len[0, 0]

    def step(t, carry):
        squares = jnp.zeros((dec, HD), jnp.float32)
        for h in range(heads):
            x_h = held[:, h * HD : (h + 1) * HD].astype(jnp.float32)
            squares = squares + x_h * x_h
        mean = jnp.sum(squares, axis=-1, keepdims=True) * (1.0 / (heads * HD))
        scale = lax.rsqrt(mean + 1e-06)
        gains = notes[t].astype(jnp.float32)
        probs = []
        for h in range(heads):
            cols = slice(h * HD, (h + 1) * HD)
            q_h = (held[:, cols].astype(jnp.float32) * scale).astype(jnp.bfloat16)
            scores = lax.dot_general(
                q_h, kv[0, :, cols], (((1,), (1,)), ((), ())),
                preferred_element_type=jnp.float32,
            ) * HD ** (-0.5)
            scores = jnp.where(key_live, scores, jnp.float32(-1e30))
            expo = jnp.exp(scores - jnp.max(scores, axis=-1, keepdims=True))
            probs.append((expo / jnp.sum(expo, axis=-1, keepdims=True)).astype(jnp.bfloat16))
        for h in range(heads):
            cols = slice(h * HD, (h + 1) * HD)
            a_h = jnp.dot(probs[h], kv[1, :, cols], preferred_element_type=jnp.float32)
            a_h = jnp.where(live, a_h, jnp.float32(0.0)).astype(jnp.bfloat16)
            mixed[t, :, cols] = a_h
            x_h = held[:, cols].astype(jnp.float32)
            moved = x_h + gains[h : h + 1, :] * a_h.astype(jnp.float32)
            held[:, cols] = moved.astype(jnp.bfloat16)
        for at, copy in mixed_copies.items():
            pl.when(t == at)(copy.start)
        return carry

    lax.fori_loop(0, STEPS, step, 0)
    final_copy.start()

    def gradient(left, right, h):
        cols = slice(h * HD, (h + 1) * HD)
        product = left[:, cols].astype(jnp.float32) * right[:, cols].astype(jnp.float32)
        return jnp.sum(product, axis=0, keepdims=True)

    for t in sorted(cot_copies, reverse=True):
        cot_copies[t].wait_recv()
        for h in range(outs[t], heads):
            part[t, h : h + 1, :] = gradient(cots.at[t], mixed.at[t], h)
        part_copies[t].start()
    for t in sorted(mixed_copies):
        own_copies[t].wait()
        mixed_copies[t].wait_recv()
        for h in range(outs[t]):
            own[t, h : h + 1, :] = gradient(own_cots.at[t], arrived.at[t], h)
    for copy in part_copies.values():
        copy.wait_recv()
    shares = []
    for t in range(STEPS):
        pieces = []
        if outs[t] > 0:
            pieces.append(own[t, : outs[t], :])
        if outs[t] < heads:
            pieces.append(parts[t, outs[t] :, :])
        shares.append(pieces[0] if len(pieces) == 1 else jnp.concatenate(pieces, axis=0))
    slots[rep] = (shares[0] + shares[1]) + shares[2]

    def slot_copy(whose, j):
        return pltpu.make_async_remote_copy(
            src_ref=slots.at[whose], dst_ref=slots.at[whose], send_sem=slot_send.at[j],
            recv_sem=slot_recv.at[whose], device_id={"dp": lax.rem(rep + j, replicas)},
            device_id_type=MESH,
        )

    def give(j, carry):
        slot_copy(rep, j).start()
        return carry

    def take(j, carry):
        slot_copy(lax.rem(rep + replicas - j, replicas), j).wait_recv()
        return carry

    lax.fori_loop(1, replicas, give, 0)
    lax.fori_loop(1, replicas, take, 0)
    total = lax.fori_loop(1, replicas, lambda r, total: total + slots[r], slots[0])
    for h in range(heads):
        grad[:, h * HD : (h + 1) * HD] = total[h : h + 1, :]

    def sent(j, carry):
        slot_copy(rep, j).wait_send()
        return carry

    lax.fori_loop(1, replicas, sent, 0)
    for copy in [
        *note_copies, *cot_copies.values(), *mixed_copies.values(), *part_copies.values()
    ]:
        copy.wait_send()
    final_copy.wait()


def window(offset, sections, replicas, states, memory, memory_len, decode_len, gain, cotangent):
    dec, width = states.shape[2:]
    enc = memory.shape[3]
    heads = width // HD
    anywhere = pl.BlockSpec(memory_space=pl.ANY)
    scalar = pl.BlockSpec(memory_space=pltpu.SMEM)
    vector = pl.BlockSpec(memory_space=pltpu.VMEM)
    dma = pltpu.SemaphoreType.DMA
    return pl.pallas_call(
        functools.partial(window_kernel, offset, sections, replicas),
        out_shape=(
            jax.ShapeDtypeStruct(states.shape, jnp.bfloat16),
            jax.ShapeDtypeStruct((1, width), jnp.float32),
        ),
        in_specs=[anywhere, anywhere, scalar, scalar, vector, anywhere],
        out_specs=(anywhere, vector),
        scratch_shapes=[
            pltpu.VMEM((2, enc, width), jnp.bfloat16),
            pltpu.VMEM((dec, width), jnp.bfloat16),
            pltpu.VMEM((STEPS, dec, width), jnp.bfloat16),
            pltpu.VMEM((STEPS, dec, width), jnp.bfloat16),
            pltpu.VMEM((STEPS, dec, width), jnp.bfloat16),
            pltpu.VMEM((STEPS, dec, width), jnp.bfloat16),
            pltpu.VMEM((2 * heads, HD), jnp.bfloat16),
            pltpu.VMEM((STEPS, 2 * heads, HD), jnp.bfloat16),
            pltpu.VMEM((2 * heads, HD), jnp.float32),
            pltpu.VMEM((STEPS, heads, HD), jnp.float32),
            pltpu.VMEM((STEPS, heads, HD), jnp.float32),
            pltpu.VMEM((STEPS, heads, HD), jnp.float32),
            pltpu.VMEM((replicas, heads, HD), jnp.float32),
            dma, dma((STEPS,)), dma, dma, dma((STEPS,)), dma((STEPS,)), dma((STEPS,)),
            dma((STEPS,)), dma((STEPS,)), dma((STEPS,)), dma((STEPS,)), dma((STEPS,)),
            dma, dma, dma((replicas,)), dma((replicas,)),
        ],
        compiler_params=pltpu.CompilerParams(
            collective_id=offset, has_side_effects=True, vmem_limit_bytes=16 * 1024 * 1024
        ),
        cost_estimate=pl.CostEstimate(
            flops=STEPS * 4 * dec * enc * width,
            bytes_accessed=2 * (2 * enc + 5 * dec) * width,
            transcendentals=STEPS * heads * dec * enc,
        ),
        name=f"window_{offset}",
    )(states, memory, memory_len, decode_len, gain, cotangent)


def solution(mesh):
    sections, replicas = mesh.shape["section"], mesh.shape["dp"]

    def per_device(states, memory, memory_len, decode_len, owner_map, section_gain, cotangent):
        branches = [
            functools.partial(window, offset, sections, replicas)
            for offset in range(STEPS, sections)
        ]
        return lax.switch(
            owner_map[0] - STEPS, branches,
            states, memory, memory_len, decode_len, section_gain, cotangent,
        )

    in_specs = (
        P("dp", "section", None, None),
        P("dp", "section", None, None, None),
        P("dp", "section"),
        P("dp", "section"),
        P(),
        P("section", None),
        P("dp", None, "section", None, None),
    )
    out_specs = (P("dp", "section", None, None), P("section", None))
    return jax.shard_map(
        per_device, mesh=mesh, in_specs=in_specs, out_specs=out_specs, check_vma=False
    )
```

profile of v0, /device:TPU:0, one launch (start us, length us, event | category | flops | bytes accessed | tf_op | source)
XLA Modules:
  0.0 63.3 jit_solution(3977677294384387099)
XLA Ops:
  1.3 60.7 %conditional.1 = ((bf16[1,1,32,4096]{3,2,1,0:T(8,128)(2,1)S(1)}, f32[1,4096]{1,0:T(1,128)S(1)})) conditional(s32[]{:T(128)} %bitcast, (bf16[1,1,32,4096]{3,2,1,0:T(8,128)(2,1)}, bf16[1,1,2,128,4096]{4,3,2,1,0:T(8,128)(2,1)}, s32[1,1]{1,0:T(1,128)}, s32[1,1]{1,0:T(1,128)}, bf16[1,4096]{1,0:T(2,128)(2,1)}, ...), branch_computations={%region_0.0_spmd, %region_1.0_spmd, %region_2.0_spmd, %region_3.0_... | conditional | flops 201326592 | bytes 3407880 | solution.py:274
  1.3 60.7 %window_5.1 = (bf16[1,1,32,4096]{3,2,1,0:T(8,128)(2,1)S(1)}, f32[1,4096]{1,0:T(1,128)S(1)}) custom-call(bf16[1,1,32,4096]{3,2,1,0:T(8,128)(2,1)} %get-tuple-element.72.states, bf16[1,1,2,128,4096]{4,3,2,1,0:T(8,128)(2,1)} %get-tuple-element.73.memory, s32[1,1]{1,0:T(1,128)} %get-tuple-element.74.memory_len, s32[1,1]{1,0:T(1,128)} %get-tuple-element.75.decode_len, ...), custom_call_target="tpu_custom_call" | custom-call | flops 201326592 | bytes 3407872 | tf_op jit(solution)/shard_map/cond/branch_2_fun/window_5/pallas_call | solution.py:228
  62.0 0.7 %copy.31 = bf16[1,1,32,4096]{3,2,1,0:T(8,128)(2,1)} copy(bf16[1,1,32,4096]{3,2,1,0:T(8,128)(2,1)S(1)} %get-tuple-element.116) | data formatting | bytes 524288
  62.7 0.6 copy.32
where the time goes:
time: 63 us; the launch traced here: 63.3 us
  Pallas kernels  60.7 us (96%)
  local copies, waits for them, and re-layouts  1.31 us (2%)
  between operations  1.29 us (2%)
    pallas_call x1, Pallas kernels, window(): pl.pallas_call(functools.partial(window_kernel, offset, sections, replica...  60.7 us
    unnamed x2, local copies, waits for them, and re-layouts  1.31 us

commit v1 on v0

--- a/solution.py
+++ b/solution.py
@@ -9,6 +9,7 @@
 
 HD = 256
 STEPS = 3
+GROUP = 4
 MESH = pl.DeviceIdType.MESH
 
 
@@ -27,7 +28,7 @@
     offset, sections, replicas,
     states, memory, memory_len, decode_len, gain, cotangent,
     final, grad,
-    kv, held, cots, own_cots, mixed, arrived, note, notes, rows_f32, part, parts, own, slots,
+    kv, keys, scores, probs, held, cots, own_cots, mixed, arrived, note, notes, rows_f32, part, parts, own, slots,
     kv_sem, own_sem, x_send, x_recv, cot_send, cot_recv, mixed_send, mixed_recv,
     note_send, note_recv, part_send, part_recv, final_send, final_recv, slot_send, slot_recv,
 ):
@@ -113,6 +114,8 @@
         cot_copies[t].start()
 
     kv_copy.wait()
+    for h in range(heads):
+        keys[h * HD : (h + 1) * HD, :] = jnp.transpose(kv[0, :, h * HD : (h + 1) * HD])
     for copy in note_copies:
         copy.wait_recv()
     x_copy.wait_recv()
@@ -121,7 +124,7 @@
 
     row = lax.broadcasted_iota(jnp.int32, (dec, HD), 0).astype(jnp.float32)
     live = row < notes[0].astype(jnp.float32)[heads : heads + 1, :]
-    key_live = lax.broadcasted_iota(jnp.int32, (dec, enc), 1) < memory_len[0, 0]
+    key_live = lax.broadcasted_iota(jnp.int32, (GROUP * dec, enc), 1) < memory_len[0, 0]
 
     def step(t, carry):
         squares = jnp.zeros((dec, HD), jnp.float32)
@@ -131,20 +134,24 @@
         mean = jnp.sum(squares, axis=-1, keepdims=True) * (1.0 / (heads * HD))
         scale = lax.rsqrt(mean + 1e-06)
         gains = notes[t].astype(jnp.float32)
-        probs = []
         for h in range(heads):
             cols = slice(h * HD, (h + 1) * HD)
             q_h = (held[:, cols].astype(jnp.float32) * scale).astype(jnp.bfloat16)
-            scores = lax.dot_general(
-                q_h, kv[0, :, cols], (((1,), (1,)), ((), ())),
-                preferred_element_type=jnp.float32,
-            ) * HD ** (-0.5)
-            scores = jnp.where(key_live, scores, jnp.float32(-1e30))
-            expo = jnp.exp(scores - jnp.max(scores, axis=-1, keepdims=True))
-            probs.append((expo / jnp.sum(expo, axis=-1, keepdims=True)).astype(jnp.bfloat16))
+            scores[h * dec : (h + 1) * dec, :] = jnp.dot(
+                q_h, keys[cols, :], preferred_element_type=jnp.float32
+            )
+        for first in range(0, heads * dec, GROUP * dec):
+            rows = slice(first, first + GROUP * dec)
+            masked = jnp.where(key_live, scores[rows, :] * HD ** (-0.5), jnp.float32(-1e30))
+            expo = jnp.exp(masked - jnp.max(masked, axis=-1, keepdims=True))
+            total = jnp.sum(expo, axis=-1, keepdims=True)
+            probs[rows, :] = (expo / total).astype(jnp.bfloat16)
         for h in range(heads):
             cols = slice(h * HD, (h + 1) * HD)
-            a_h = jnp.dot(probs[h], kv[1, :, cols], preferred_element_type=jnp.float32)
+            a_h = jnp.dot(
+                probs[h * dec : (h + 1) * dec, :], kv[1, :, cols],
+                preferred_element_type=jnp.float32,
+            )
             a_h = jnp.where(live, a_h, jnp.float32(0.0)).astype(jnp.bfloat16)
             mixed[t, :, cols] = a_h
             x_h = held[:, cols].astype(jnp.float32)
@@ -235,6 +242,9 @@
         out_specs=(anywhere, vector),
         scratch_shapes=[
             pltpu.VMEM((2, enc, width), jnp.bfloat16),
+            pltpu.VMEM((width, enc), jnp.bfloat16),
+            pltpu.VMEM((heads * dec, enc), jnp.float32),
+            pltpu.VMEM((heads * dec, enc), jnp.bfloat16),
             pltpu.VMEM((dec, width), jnp.bfloat16),
             pltpu.VMEM((STEPS, dec, width), jnp.bfloat16),
             pltpu.VMEM((STEPS, dec, width), jnp.bfloat16),

time: 63 us -> 65.6 us (1.041)
  the two profiles are of different devices: /device:TPU:0 before, /device:TPU:27 now
where the time goes in v1:
time: 65.6 us; the launch traced here: 65.4 us
  Pallas kernels  62.7 us (96%)
  local copies, waits for them, and re-layouts  1.31 us (2%)
  between operations  1.29 us (2%)
    pallas_call x1, Pallas kernels, window(): pl.pallas_call(functools.partial(window_kernel, offset, sections, replica...  62.7 us

profile of v1, /device:TPU:27, one launch (start us, length us, event | category | flops | bytes accessed | tf_op | source)
XLA Modules:
  0.0 65.4 jit_solution(2063727940551923385)
XLA Ops:
  1.3 62.8 %conditional.1 = ((bf16[1,1,32,4096]{3,2,1,0:T(8,128)(2,1)S(1)}, f32[1,4096]{1,0:T(1,128)S(1)})) conditional(s32[]{:T(128)} %bitcast, (bf16[1,1,32,4096]{3,2,1,0:T(8,128)(2,1)}, bf16[1,1,2,128,4096]{4,3,2,1,0:T(8,128)(2,1)}, s32[1,1]{1,0:T(1,128)}, s32[1,1]{1,0:T(1,128)}, bf16[1,4096]{1,0:T(2,128)(2,1)}, ...), branch_computations={%region_0.0_spmd, %region_1.0_spmd, %region_2.0_spmd, %region_3.0_... | conditional | flops 201326592 | bytes 3407880 | solution.py:284
  1.3 62.7 %window_5.1 = (bf16[1,1,32,4096]{3,2,1,0:T(8,128)(2,1)S(1)}, f32[1,4096]{1,0:T(1,128)S(1)}) custom-call(bf16[1,1,32,4096]{3,2,1,0:T(8,128)(2,1)} %get-tuple-element.72.states, bf16[1,1,2,128,4096]{4,3,2,1,0:T(8,128)(2,1)} %get-tuple-element.73.memory, s32[1,1]{1,0:T(1,128)} %get-tuple-element.74.memory_len, s32[1,1]{1,0:T(1,128)} %get-tuple-element.75.decode_len, ...), custom_call_target="tpu_custom_call" | custom-call | flops 201326592 | bytes 3407872 | tf_op jit(solution)/shard_map/cond/branch_2_fun/window_5/pallas_call | solution.py:235
  64.1 0.7 %copy.31 = bf16[1,1,32,4096]{3,2,1,0:T(8,128)(2,1)} copy(bf16[1,1,32,4096]{3,2,1,0:T(8,128)(2,1)S(1)} %get-tuple-element.116) | data formatting | bytes 524288
  64.8 0.6 copy.32
